TPU v7x, 32 devices: a whole 2x2x4 slice. The times are simulated.
32 devices in a mesh: groups: 2 (over x), cx: 16 (over z, y, core).
Axes of the slice: x: 2, y: 2, z: 4, core: 2. Of those that a mesh axis runs over, the one named last changes fastest.
Arguments:
- displacements: bfloat16 [512, 3, 5120], P(('groups', 'cx')), parts along dimension 0, may hold values from -6 to 6
- forces: bfloat16 [512, 3, 5120], P(('groups', 'cx')), parts along dimension 0, may hold values from -6 to 6
- phi: bfloat16 [160, 14, 192, 192], P(('groups', 'cx')), parts along dimension 0, may hold values from -0.125 to 0.125
- neighbours: int32 [80, 14], P('cx'), may hold values from 0 to 79, as said below
- cluster_atoms: int32 [80, 64], P('cx'), may hold values from 0 to 5119, as said below
- config_order: int32 [512], P('groups'), parts along dimension 0, may hold values from 0 to 255, each once
- weights: float32 [512], P('groups'), parts along dimension 0, may hold values from 0.02 to 0.3
Outputs:
- residual: bfloat16 [160, 192, 256], P(('groups', 'cx')), parts along dimension 0
- gradient: bfloat16 [160, 14, 192, 192], P(('groups', 'cx')), parts along dimension 0
There are 2 independent parts, one for each index of `groups`. A program takes and returns all parts, laid end to end along the dimension named above; an argument that names none is the same for every part. Nothing has to cross between parts.
Inputs may be any that keep to these rules, and one draw needn't show every extreme that they name: `neighbours`: cluster c lies in layer c // 5 of 16 periodic layers; its 14 blocks name distinct clusters of its own layer and the two layers beside it, wrapping at the ends. `cluster_atoms`: the clusters of layer j hold the atoms 5 * 64 * j to 5 * 64 * (j + 1) - 1, each once. `config_order`: each ensemble index once.
All inputs are finite; a program needn't handle non-finite values.
Results may differ from a plain program's by a relative error of at most 0.0085.
Values may be sent and summed in bfloat16 or wider, within the bound.
A program may use at most 128 MiB of HBM per device.

v0:
```python
import jax
import jax.numpy as jnp
from jax import lax
from jax.sharding import PartitionSpec as P

ATOMS = 64
LAYER = 5


def with_halo(block, sides, width):
    for axis, dim in sides:
        count = lax.axis_size(axis)
        forward = [(i, i + 1) for i in range(count - 1)]
        forward.append((count - 1, 0))
        backward = [(target, source) for source, target in forward]
        low = lax.ppermute(
            lax.slice_in_dim(block, block.shape[dim] - width, None, axis=dim), axis, forward
        )
        high = lax.ppermute(lax.slice_in_dim(block, 0, width, axis=dim), axis, backward)
        block = jnp.concatenate([low, block, high], axis=dim)
    return block


def arrange(field, atom_map):
    picked = jnp.take(field, atom_map.reshape(-1), axis=2)
    picked = picked.reshape(field.shape[0], 3, atom_map.shape[0], atom_map.shape[1])
    return jnp.transpose(picked, (2, 1, 3, 0)).reshape(
        atom_map.shape[0], 3 * atom_map.shape[1], field.shape[0]
    )


def shards(displacements, forces, phi, neighbours, cluster_atoms, config_order, weights):
    axis_width = lax.axis_size("cx")
    position = lax.axis_index("cx")
    atom_local = cluster_atoms - position * (LAYER * ATOMS)
    layer_of = neighbours // LAYER
    offset = (layer_of - position + 1 + axis_width) % axis_width
    near_index = offset * LAYER + neighbours % LAYER
    moved_disp, moved_force = (
        lax.all_to_all(displacements, "cx", split_axis=2, concat_axis=0, tiled=True),
        lax.all_to_all(forces, "cx", split_axis=2, concat_axis=0, tiled=True),
    )
    cluster_force = arrange(moved_force, atom_local)
    cluster_disp = arrange(moved_disp, atom_local)
    framed_disp = with_halo(cluster_disp, (("cx", 0),), LAYER)
    beside_disp = jnp.take(framed_disp, near_index, axis=0)
    harmonic = jnp.einsum("ckij,ckjs->cis", phi, beside_disp, preferred_element_type=jnp.float32)
    residual = (cluster_force.astype(jnp.float32) + harmonic).astype(jnp.bfloat16)
    framed_resid = with_halo(residual, (("cx", 0),), LAYER)
    beside_resid = jnp.take(framed_resid, near_index, axis=0)
    match = config_order[:, None] == jnp.arange(config_order.shape[0], dtype=jnp.int32)[None, :]
    weight_row = jnp.sum(
        jnp.where(match, weights[None, :], jnp.zeros_like(weights)[None, :]), axis=1
    )
    wres = (residual.astype(jnp.float32) * weight_row[None, None, :]).astype(jnp.bfloat16)
    wdisp = (cluster_disp.astype(jnp.float32) * weight_row[None, None, :]).astype(jnp.bfloat16)
    first = jnp.einsum("cis,ckjs->ckij", wres, beside_disp, preferred_element_type=jnp.float32)
    second = jnp.einsum("cis,ckjs->ckij", wdisp, beside_resid, preferred_element_type=jnp.float32)
    summed = first + second
    gradient = (0.5 * summed).astype(jnp.bfloat16)
    return (residual, gradient)


def solution(mesh):
    in_specs = (
        P(("groups", "cx"), None, None),
        P(("groups", "cx"), None, None),
        P(("groups", "cx"), None, None, None),
        P("cx", None),
        P("cx", None),
        P("groups"),
        P("groups"),
    )
    out_specs = (P(("groups", "cx"), None, None), P(("groups", "cx"), None, None, None))
    return jax.shard_map(shards, mesh=mesh, in_specs=in_specs, out_specs=out_specs, check_vma=False)
```

profile of v0, /device:TPU:0, one launch (start us, length us, event | category | flops | bytes accessed | tf_op | source)
XLA Modules:
  0.0 138.1 jit_solution(12460175650179497296)
XLA Ops:
  0.6 0.0 copy-start.3
  0.6 0.0 copy-start.2
  0.6 6.5 %copy.46 = bf16[16,3,5120]{0,1,2:T(4,128)(2,1)} copy(bf16[16,3,5120]{2,0,1:T(8,128)(2,1)} %param.11) | data formatting | bytes 983040 | tf_op args[0]
  7.1 8.1 %reshape.93 = bf16[16,2,7680]{2,1,0:T(2,128)(2,1)} reshape(bf16[5120,3,16]{2,1,0:T(4,128)(2,1)} %bitcast.54) | data formatting | bytes 983040
  15.2 0.0 copy-start.4
  15.2 0.0 copy-start.5
  15.2 0.0 copy-start.6
  15.2 7.5 %all-to-all-start.1 = ((bf16[16,2,7680]{2,1,0:T(2,128)(2,1)}), bf16[16,2,7680]{2,1,0:T(2,128)(2,1)S(1)}, u32[]{:S(2)}, u32[]{:S(2)}) async-start(bf16[16,2,7680]{2,1,0:T(2,128)(2,1)} %reshape.93), calls=%async_computation.1 | async-start | bytes 983040 | tf_op jit(solution)/shard_map/all_to_all | solution.py:40
  22.8 0.0 copy-done.3
  22.8 0.1 reshape.33
  22.9 0.0 copy-done.2
  22.9 4.9 %copy.41 = bf16[16,3,5120]{0,1,2:T(4,128)(2,1)} copy(bf16[16,3,5120]{2,0,1:T(8,128)(2,1)S(1)} %copy-done.2) | data formatting | bytes 983040 | tf_op args[1]
  27.8 8.1 %reshape.91 = bf16[16,2,7680]{2,1,0:T(2,128)(2,1)} reshape(bf16[5120,3,16]{2,1,0:T(4,128)(2,1)} %bitcast.55) | data formatting | bytes 983040
  35.9 0.0 copy-done.4
  35.9 0.6 all-to-all-done.1
  36.5 5.4 %all-to-all-start = ((bf16[16,2,7680]{2,1,0:T(2,128)(2,1)}), bf16[16,2,7680]{2,1,0:T(2,128)(2,1)S(1)}, u32[]{:S(2)}, u32[]{:S(2)}) async-start(bf16[16,2,7680]{2,1,0:T(2,128)(2,1)} %reshape.91), calls=%async_computation | async-start | bytes 983040 | tf_op jit(solution)/shard_map/all_to_all | solution.py:41
  42.0 0.1 reshape.80
  42.1 0.0 copy-done.5
  42.1 0.0 copy-done.6
  42.1 0.2 select_reduce_fusion
  42.3 6.4 %reshape.94 = bf16[5120,3,16]{2,1,0:T(4,128)(2,1)} reshape(bf16[16,2,7680]{2,1,0:T(2,128)(2,1)S(1)} %all-to-all-done.1) | data formatting | bytes 983040
  48.7 5.9 %copy.47 = bf16[16,3,16,320]{3,0,2,1:T(8,128)(2,1)S(1)} copy(bf16[16,3,16,320]{0,1,3,2:T(4,128)(2,1)} %bitcast.52) | data formatting | bytes 983040 | tf_op jit(solution)/shard_map/all_to_all | solution.py:40
  54.6 0.7 copy.48
  55.3 2.3 %gather_fusion.1 = bf16[320,256,3]{1,2,0:T(4,128)(2,1)S(1)} fusion(bf16[256,3,320]{0,1,2:T(4,128)(2,1)S(1)} %copy.48, s32[1024]{0:T(1024)S(1)} %pad_clamp_fusion.1), kind=kCustom, calls=%fused_computation.2.clone | custom fusion | bytes 984320 | tf_op jit(solution)/shard_map/jit(_take)/gather | solution.py:25
  57.6 1.1 select_bitcast_fusion
  58.8 0.1 copy.49
  58.9 4.4 %collective-permute-start.1 = (bf16[5,192,256]{2,1,0:T(8,128)(2,1)S(1)}, bf16[5,192,256]{2,1,0:T(8,128)(2,1)}, u32[]{:S(2)}, u32[]{:S(2)}) collective-permute-start(bf16[5,192,256]{2,1,0:T(8,128)(2,1)S(1)} %bitcast.56), channel_id=1, source_target_pairs={{1,0},{2,1},{3,2},{4,3},{5,4},{6,5},{7,6},{8,7},{9,8},{10,9},{11,1... | collective-permute-start | bytes 1474568 | tf_op jit(solution)/shard_map/ppermute | solution.py:19
  63.3 0.0 collective-permute-start
  63.3 0.0 all-to-all-done
  63.3 6.4 %reshape.92 = bf16[5120,3,16]{2,1,0:T(4,128)(2,1)} reshape(bf16[16,2,7680]{2,1,0:T(2,128)(2,1)S(1)} %all-to-all-done) | data formatting | bytes 983040
  69.7 5.9 %copy.42 = bf16[16,3,16,320]{3,0,2,1:T(8,128)(2,1)S(1)} copy(bf16[16,3,16,320]{0,1,3,2:T(4,128)(2,1)} %bitcast.53) | data formatting | bytes 983040 | tf_op jit(solution)/shard_map/all_to_all | solution.py:41
  75.6 0.7 copy.43
  76.3 2.3 %gather_fusion = bf16[320,256,3]{1,2,0:T(4,128)(2,1)S(1)} fusion(bf16[256,3,320]{0,1,2:T(4,128)(2,1)S(1)} %copy.43, s32[1024]{0:T(1024)S(1)} %pad_clamp_fusion.1), kind=kCustom, calls=%fused_computation.clone | custom fusion | bytes 984320 | tf_op jit(solution)/shard_map/jit(_take)/gather | solution.py:25
  78.6 0.1 copy_select_fusion
  78.7 0.1 convert_bitcast_fusion
  78.8 0.1 copy.45
  78.9 0.0 collective-permute-done.1
  78.9 0.0 collective-permute-done
  78.9 1.3 pad_maximum_fusion
  80.3 6.7 %gather_fusion.2 = bf16[70,192,256]{2,1,0:T(8,128)(2,1)} fusion(bf16[15,192,256]{2,1,0:T(8,128)(2,1)S(1)} %pad_maximum_fusion, s32[1024]{0:T(1024)S(1)} %pad_clamp_fusion), kind=kCustom, calls=%fused_computation.1.clone | custom fusion | bytes 13762840 | tf_op jit(solution)/shard_map/jit(_take)/gather | solution.py:46
  87.0 0.0 copy-start
  87.0 7.2 %fusion.12 = bf16[5,192,256]{2,1,0:T(8,128)(2,1)S(1)} fusion(f32[5,192,256]{2,1,0:T(8,128)S(1)} %bitcast.64, bf16[5,14,192,192]{3,2,1,0:T(8,128)(2,1)} %param.13, bf16[5,14,192,256]{3,2,1,0:T(8,128)(2,1)} %bitcast.50, pred[5,14]{1,0:T(8,128)(4,1)S(1)} %get-tuple-element.14), kind=kOutput, calls=%fused_computation.18 | convolution fusion | flops 1325137920 | bytes 13516870 | tf_op jit(solution)/shard_map/ckij,ckjs->cis/dot_general | solution.py:47
  94.2 0.0 copy-start.1
  94.2 4.5 %collective-permute-start.3 = (bf16[5,192,256]{2,1,0:T(8,128)(2,1)S(1)}, bf16[5,192,256]{2,1,0:T(8,128)(2,1)S(1)}, u32[]{:S(2)}, u32[]{:S(2)}) collective-permute-start(bf16[5,192,256]{2,1,0:T(8,128)(2,1)S(1)} %fusion.12), channel_id=1, source_target_pairs={{1,0},{2,1},{3,2},{4,3},{5,4},{6,5},{7,6},{8,7},{9,8},{10,9},{11,1... | collective-permute-start | bytes 1474568 | tf_op jit(solution)/shard_map/ppermute | solution.py:19
  98.7 0.0 collective-permute-start.2
  98.7 0.0 copy-done
  98.7 7.0 %fusion.2 = f32[5,14,192,192]{3,2,1,0:T(8,128)} fusion(bf16[5,14,192,256]{3,2,1,0:T(8,128)(2,1)S(1)} %bitcast.51, pred[5,14]{1,0:T(8,128)(4,1)S(1)} %get-tuple-element.14, bf16[5,192,256]{2,1,0:T(8,128)(2,1)S(1)} %fusion.12, f32[256]{0:T(256)S(1)} %select_reduce_fusion), kind=kOutput, calls=%fused_computation.8 | convolution fusion | flops 1325383680 | bytes 17695814 | tf_op jit(solution)/shard_map/cis,ckjs->ckij/dot_general | solution.py:57
  105.7 0.0 collective-permute-done.3
  105.7 4.0 %collective-permute-done.2 = bf16[5,192,256]{2,1,0:T(8,128)(2,1)S(1)} collective-permute-done((bf16[5,192,256]{2,1,0:T(8,128)(2,1)S(1)}, bf16[5,192,256]{2,1,0:T(8,128)(2,1)S(1)}, u32[]{:S(2)}, u32[]{:S(2)}) %collective-permute-start.2) | collective-permute-done | bytes 491552 | tf_op jit(solution)/shard_map/ppermute | solution.py:16
  109.6 0.0 copy-done.1
  109.6 0.2 pad_maximum_fusion.1
  109.8 6.7 %gather_fusion.3 = bf16[70,192,256]{2,1,0:T(8,128)(2,1)} fusion(bf16[15,192,256]{2,1,0:T(8,128)(2,1)S(1)} %pad_maximum_fusion.1, s32[1024]{0:T(1024)S(1)} %pad_clamp_fusion), kind=kCustom, calls=%fused_computation.3.clone | custom fusion | bytes 13762840 | tf_op jit(solution)/shard_map/jit(_take)/gather | solution.py:50
  116.5 11.6 %fusion.4 = bf16[5,14,192,192]{2,3,1,0:T(8,128)(2,1)} fusion(f32[5,14,192,192]{3,2,1,0:T(8,128)} %fusion.2, bf16[5,14,192,256]{3,2,1,0:T(8,128)(2,1)} %bitcast.49, pred[5,14]{1,0:T(8,128)(4,1)S(1)} %get-tuple-element.14, bf16[5,192,256]{2,1,0:T(8,128)(2,1)S(1)} %bitcast.59, f32[256]{0:T(256)S(1)} %select_reduce_fusion), kind=kOutput, calls=%fused_computation.10 | convolution fusion | flops 1333125120 | bytes 22856774 | tf_op jit(solution)/shard_map/cis,ckjs->ckij/dot_general | solution.py:58
  128.2 10.0 %copy.51 = bf16[5,14,192,192]{3,2,1,0:T(8,128)(2,1)} copy(bf16[5,14,192,192]{2,3,1,0:T(8,128)(2,1)} %fusion.4) | data formatting | bytes 10321920
  (7 shorter events, 0.1 us)
Async XLA Ops:
  0.6 22.1 %copy-start.3 = (s32[5,64]{1,0:T(8,128)S(1)}, s32[5,64]{1,0:T(8,128)}, u32[]{:S(2)}) copy-start(s32[5,64]{1,0:T(8,128)} %param.15) | copy-start | bytes 3844
  0.6 22.2 %copy-start.2 = (bf16[16,3,5120]{2,0,1:T(8,128)(2,1)S(1)}, bf16[16,3,5120]{2,0,1:T(8,128)(2,1)}, u32[]{:S(2)}) copy-start(bf16[16,3,5120]{2,0,1:T(8,128)(2,1)} %param.12) | copy-start | bytes 1474564
  15.2 20.7 %copy-start.4 = (s32[5,14]{1,0:T(8,128)S(1)}, s32[5,14]{1,0:T(8,128)}, u32[]{:S(2)}) copy-start(s32[5,14]{1,0:T(8,128)} %param.14) | copy-start | bytes 844
  15.2 26.9 %copy-start.5 = (f32[256]{0:T(256)S(1)}, f32[256]{0:T(256)}, u32[]{:S(2)}) copy-start(f32[256]{0:T(256)} %param.17) | copy-start | bytes 3076
  15.2 26.9 %copy-start.6 = (s32[256]{0:T(256)S(1)}, s32[256]{0:T(256)}, u32[]{:S(2)}) copy-start(s32[256]{0:T(256)} %param.16) | copy-start | bytes 3076
  15.2 21.3 %all-to-all-start.1 = ((bf16[16,2,7680]{2,1,0:T(2,128)(2,1)}), bf16[16,2,7680]{2,1,0:T(2,128)(2,1)S(1)}, u32[]{:S(2)}, u32[]{:S(2)}) async-start(bf16[16,2,7680]{2,1,0:T(2,128)(2,1)} %reshape.93), calls=%async_computation.1 | async-start | bytes 983040 | tf_op jit(solution)/shard_map/all_to_all | solution.py:40
  36.5 26.8 %all-to-all-start = ((bf16[16,2,7680]{2,1,0:T(2,128)(2,1)}), bf16[16,2,7680]{2,1,0:T(2,128)(2,1)S(1)}, u32[]{:S(2)}, u32[]{:S(2)}) async-start(bf16[16,2,7680]{2,1,0:T(2,128)(2,1)} %reshape.91), calls=%async_computation | async-start | bytes 983040 | tf_op jit(solution)/shard_map/all_to_all | solution.py:41
  58.9 20.1 %collective-permute-start.1 = (bf16[5,192,256]{2,1,0:T(8,128)(2,1)S(1)}, bf16[5,192,256]{2,1,0:T(8,128)(2,1)}, u32[]{:S(2)}, u32[]{:S(2)}) collective-permute-start(bf16[5,192,256]{2,1,0:T(8,128)(2,1)S(1)} %bitcast.56), channel_id=1, source_target_pairs={{1,0},{2,1},{3,2},{4,3},{5,4},{6,5},{7,6},{8,7},{9,8},{10,9},{11,1... | collective-permute-start | bytes 1474568 | tf_op jit(solution)/shard_map/ppermute | solution.py:19
  63.3 15.6 %collective-permute-start = (bf16[5,192,256]{2,1,0:T(8,128)(2,1)S(1)}, bf16[5,192,256]{2,1,0:T(8,128)(2,1)}, u32[]{:S(2)}, u32[]{:S(2)}) collective-permute-start(bf16[5,192,256]{2,1,0:T(8,128)(2,1)S(1)} %bitcast.57), channel_id=1, source_target_pairs={{0,1},{1,2},{2,3},{3,4},{4,5},{5,6},{6,7},{7,8},{8,9},{9,10},{10,1... | collective-permute-start | bytes 1474568 | tf_op jit(solution)/shard_map/ppermute | solution.py:16
  87.0 11.7 %copy-start = (bf16[70,192,256]{2,1,0:T(8,128)(2,1)S(1)}, bf16[70,192,256]{2,1,0:T(8,128)(2,1)}, u32[]{:S(2)}) copy-start(bf16[70,192,256]{2,1,0:T(8,128)(2,1)} %gather_fusion.2) | copy-start | bytes 20643844
  94.2 15.5 %copy-start.1 = (bf16[5,192,256]{2,1,0:T(8,128)(2,1)}, bf16[5,192,256]{2,1,0:T(8,128)(2,1)S(1)}, u32[]{:S(2)}) copy-start(bf16[5,192,256]{2,1,0:T(8,128)(2,1)S(1)} %fusion.12) | copy-start | bytes 1474564
  94.2 11.5 %collective-permute-start.3 = (bf16[5,192,256]{2,1,0:T(8,128)(2,1)S(1)}, bf16[5,192,256]{2,1,0:T(8,128)(2,1)S(1)}, u32[]{:S(2)}, u32[]{:S(2)}) collective-permute-start(bf16[5,192,256]{2,1,0:T(8,128)(2,1)S(1)} %fusion.12), channel_id=1, source_target_pairs={{1,0},{2,1},{3,2},{4,3},{5,4},{6,5},{7,6},{8,7},{9,8},{10,9},{11,1... | collective-permute-start | bytes 1474568 | tf_op jit(solution)/shard_map/ppermute | solution.py:19
  98.7 11.0 %collective-permute-start.2 = (bf16[5,192,256]{2,1,0:T(8,128)(2,1)S(1)}, bf16[5,192,256]{2,1,0:T(8,128)(2,1)S(1)}, u32[]{:S(2)}, u32[]{:S(2)}) collective-permute-start(bf16[5,192,256]{2,1,0:T(8,128)(2,1)S(1)} %fusion.12), channel_id=1, source_target_pairs={{0,1},{1,2},{2,3},{3,4},{4,5},{5,6},{6,7},{7,8},{8,9},{9,10},{10,1... | collective-permute-start | bytes 1474568 | tf_op jit(solution)/shard_map/ppermute | solution.py:16
where the time goes:
time: 140 us; the launch traced here: 138 us
  local copies, waits for them, and re-layouts  82 us (59%)
  matrix products  25.8 us (18%)
  starting transfers between devices  21.9 us (16%)
  waiting for transfers between devices  4.59 us (3%)
  other arithmetic  3.08 us (2%)
    unnamed x21, local copies, waits for them, and re-layouts  50.4 us
    dot_general x1, matrix products, shards(): jnp.einsum('cis,ckjs->ckij', wdisp, beside_resid, preferred_element_type=...  11.6 us
    ppermute x2, starting transfers between devices, with_halo(): lax.ppermute(lax.slice_in_dim(block, 0, width, axis=dim), axis, backward)  8.92 us
    all_to_all x1, starting transfers between devices, shards(): lax.all_to_all(displacements, 'cx', split_axis=2, concat_axis=0, tiled=True)  7.52 us
    dot_general x1, matrix products, shards(): jnp.einsum('ckij,ckjs->cis', phi, beside_disp, preferred_element_type=jnp...  7.16 us
    dot_general x1, matrix products, shards(): jnp.einsum('cis,ckjs->ckij', wres, beside_disp, preferred_element_type=jn...  6.97 us
    gather x1, local copies, waits for them, and re-layouts, shards(): beside_disp = jnp.take(framed_disp, near_index, axis=0)  6.73 us
    gather x1, local copies, waits for them, and re-layouts, shards(): beside_resid = jnp.take(framed_resid, near_index, axis=0)  6.73 us
  transfers between devices with their start and end apart: 6, of which 2 were waited for; matrix products, arithmetic and copies ran while one was open for 38% of the time, Pallas kernels for 0%

commit v1 on v0

v1 whole, which is shorter than its diff:
```python
import functools

import jax
import jax.numpy as jnp
from jax import lax
from jax.experimental import pallas as pl
from jax.experimental.pallas import tpu as pltpu
from jax.sharding import PartitionSpec as P

LANES = 128
SUBLANES = 16
ANY = pl.BlockSpec(memory_space=pl.ANY)
VMEM = pl.BlockSpec(memory_space=pltpu.VMEM)
SMEM = pl.BlockSpec(memory_space=pltpu.SMEM)
NT = (((1,), (1,)), ((), ()))


def column(row):
    m = row.shape[1]
    eye = lax.broadcasted_iota(jnp.int32, (m, m), 0) == lax.broadcasted_iota(
        jnp.int32, (m, m), 1
    )
    return jnp.sum(jnp.where(eye, row, jnp.zeros_like(row)), axis=1, keepdims=True)


def exchange(
    n, rows, span,
    disp, force, phi, near, atoms, order, weights,
    frame_disp, frame_resid, sides,
    phi_v, got_disp, got_force, pick, cdisp, cforce, resid, wt,
    own_sem, phi_sem, send_sem, recv_sem, halo_send, halo_recv, back_send, back_recv, out_sem,
):
    layer, size = atoms.shape
    blocks = phi.shape[1]
    padded, width = got_disp.shape[2:]
    me = lax.axis_index("cx")
    right, left = lax.rem(me + 1, n), lax.rem(me + n - 1, n)

    def start_of(owner):
        return pl.multiple_of((owner * span) // LANES * LANES, LANES)

    phi_copies = [
        pltpu.make_async_copy(phi.at[c], phi_v.at[c], phi_sem.at[c]) for c in range(layer)
    ]
    fields = ((disp, got_disp), (force, got_force))
    own_copies = [
        pltpu.make_async_copy(src.at[:, :, pl.ds(start_of(me), width)], dst.at[me], own_sem.at[i])
        for i, (src, dst) in enumerate(fields)
    ]

    barrier = pltpu.get_barrier_semaphore()

    @pl.loop(1, n)
    def _(i):
        pl.semaphore_signal(barrier, inc=1, device_id={"cx": lax.rem(me + i, n)})

    for copy in own_copies:
        copy.start()

    shift = me * span - (me * span) // LANES * LANES
    for c in range(layer):
        place = column((atoms[c : c + 1, :] - me * span + shift).astype(jnp.float32))
        lane = lax.broadcasted_iota(jnp.int32, (size, width), 1).astype(jnp.float32)
        pick[c * size : (c + 1) * size, :] = jnp.where(lane == place, 1.0, 0.0).astype(jnp.bfloat16)
    configs = order.shape[1]
    match = order[...] == lax.broadcasted_iota(jnp.int32, (configs, configs), 0)
    wt[...] = jnp.sum(jnp.where(match, column(weights[...]), 0.0), axis=0, keepdims=True)

    pl.semaphore_wait(barrier, n - 1)

    def moved(field, i, owner):
        src, dst = fields[field]
        peer = lax.rem(me + i, n)
        return pltpu.make_async_remote_copy(
            src_ref=src.at[:, :, pl.ds(start_of(peer), width)],
            dst_ref=dst.at[owner],
            send_sem=send_sem.at[field, i],
            recv_sem=recv_sem.at[field, i],
            device_id={"cx": peer},
        )

    for field in range(2):

        @pl.loop(1, n)
        def _(i):
            moved(field, i, me).start()

    for copy in phi_copies:
        copy.start()

    def gathered(field, store):
        own_copies[field].wait()

        @pl.loop(1, n)
        def _(i):
            moved(field, i, lax.rem(me + n - i, n)).wait_recv()

        for a in range(3):
            x = fields[field][1][:, a].reshape(n * padded, width)
            y = lax.dot_general(pick[...], x, NT, preferred_element_type=jnp.float32)
            if padded != rows:
                sub = lax.broadcasted_iota(jnp.int32, (n * padded, n * rows), 0)
                col = lax.broadcasted_iota(jnp.int32, (n * padded, n * rows), 1)
                keep = sub == col // rows * padded + col % rows
                y = jnp.dot(
                    y.astype(jnp.bfloat16),
                    jnp.where(keep, 1.0, 0.0).astype(jnp.bfloat16),
                    preferred_element_type=jnp.float32,
                )
            for c in range(layer):
                store(c, a, y[c * size : (c + 1) * size, :])

    def keep_disp(c, a, value):
        cdisp[layer + c, a * size : (a + 1) * size, :] = value.astype(jnp.bfloat16)

    def keep_force(c, a, value):
        cforce[c, a * size : (a + 1) * size, :] = value

    gathered(0, keep_disp)
    middle = pl.ds(layer, layer)
    halo = [
        pltpu.make_async_remote_copy(
            src_ref=cdisp.at[middle],
            dst_ref=cdisp.at[pl.ds(place, layer)],
            send_sem=halo_send.at[i],
            recv_sem=halo_recv.at[i],
            device_id={"cx": peer},
        )
        for i, (peer, place) in enumerate(((right, 0), (left, 2 * layer)))
    ]
    for copy in halo:
        copy.start()
    gathered(1, keep_force)
    for copy in halo:
        copy.wait_recv()
    disp_out = pltpu.make_async_copy(cdisp, frame_disp, out_sem.at[0])
    disp_out.start()
    for copy in phi_copies:
        copy.wait()

    def back(c, side):
        peer, place = ((right, 0), (left, 2 * layer))[side]
        return pltpu.make_async_remote_copy(
            src_ref=resid.at[c],
            dst_ref=frame_resid.at[place + c],
            send_sem=back_send.at[side, c],
            recv_sem=back_recv.at[side, c],
            device_id={"cx": peer},
        )

    def keep(c):
        return pltpu.make_async_copy(resid.at[c], frame_resid.at[layer + c], out_sem.at[1 + c])

    dof = 3 * size

    @pl.loop(0, layer)
    def _(c):
        total = cforce[c]
        for k in range(blocks):
            name = near[c, k]
            offset = jnp.minimum(lax.rem(name // layer - me + 1 + n, n), 2)
            total += jnp.dot(
                phi_v[c, k],
                cdisp[offset * layer + lax.rem(name, layer)],
                preferred_element_type=jnp.float32,
            )
        rounded = total.astype(jnp.bfloat16)
        resid[c] = rounded
        back(c, 0).start()
        back(c, 1).start()
        keep(c).start()
        sides[c, :, :configs] = (rounded.astype(jnp.float32) * wt[...]).astype(jnp.bfloat16)
        sides[c, :, configs:] = (cdisp[layer + c].astype(jnp.float32) * wt[...]).astype(
            jnp.bfloat16
        )

    for field in range(2):

        @pl.loop(1, n)
        def _(i):
            moved(field, i, me).wait_send()

    for copy in halo:
        copy.wait_send()
    disp_out.wait()
    for c in range(layer):
        keep(c).wait()
        for side in range(2):
            back(c, side).wait()


def products(n, layer, near, position, sides, disp, resid, residual, gradient):
    c = pl.program_id(0)
    blocks = gradient.shape[1]
    configs = disp.shape[2]
    me = position[0]
    residual[0] = resid[layer + c]
    for k in range(blocks):
        name = near[c, k]
        offset = jnp.minimum(lax.rem(name // layer - me + 1 + n, n), 2)
        index = offset * layer + lax.rem(name, layer)
        total = lax.dot_general(
            sides[0, :, :configs], disp[index], NT, preferred_element_type=jnp.float32
        ) + lax.dot_general(
            sides[0, :, configs:], resid[index], NT, preferred_element_type=jnp.float32
        )
        gradient[0, k] = (0.5 * total).astype(jnp.bfloat16)


def shards(n, displacements, forces, phi, neighbours, cluster_atoms, config_order, weights):
    rows, _, atoms = displacements.shape
    layer, size = cluster_atoms.shape
    blocks, dof = phi.shape[1:3]
    configs = config_order.shape[0]
    span = atoms // n
    width = -(-span // LANES) * LANES
    while any((p * span) % LANES + span > width for p in range(n)):
        width += LANES
    padded = -(-rows // SUBLANES) * SUBLANES

    def laid(field):
        field = jnp.transpose(field, (1, 0, 2))
        if padded != rows:
            field = jnp.pad(field, ((0, 0), (0, padded - rows), (0, 0)))
        return field

    bf16 = jnp.bfloat16
    dma = pltpu.SemaphoreType.DMA
    frame = jax.ShapeDtypeStruct((3 * layer, dof, configs), bf16)
    frame_disp, frame_resid, sides = pl.pallas_call(
        functools.partial(exchange, n, rows, span),
        out_shape=[frame, frame, jax.ShapeDtypeStruct((layer, dof, 2 * configs), bf16)],
        in_specs=[ANY, ANY, ANY, SMEM, VMEM, VMEM, VMEM],
        out_specs=[ANY, ANY, VMEM],
        scratch_shapes=[
            pltpu.VMEM(phi.shape, bf16),
            pltpu.VMEM((n, 3, padded, width), bf16),
            pltpu.VMEM((n, 3, padded, width), bf16),
            pltpu.VMEM((layer * size, width), bf16),
            pltpu.VMEM((3 * layer, dof, configs), bf16),
            pltpu.VMEM((layer, dof, configs), jnp.float32),
            pltpu.VMEM((layer, dof, configs), bf16),
            pltpu.VMEM((1, configs), jnp.float32),
            dma((2,)),
            dma((layer,)),
            dma((2, n)),
            dma((2, n)),
            dma((2,)),
            dma((2,)),
            dma((2, layer)),
            dma((2, layer)),
            dma((1 + layer,)),
        ],
        compiler_params=pltpu.CompilerParams(
            collective_id=0, has_side_effects=True, vmem_limit_bytes=32 * 1024 * 1024
        ),
    )(
        laid(displacements),
        laid(forces),
        phi,
        neighbours,
        cluster_atoms,
        config_order.reshape(1, configs),
        weights.reshape(1, configs),
    )
    position = lax.axis_index("cx").reshape(1).astype(jnp.int32)
    whole = pl.BlockSpec((3 * layer, dof, configs), lambda c: (0, 0, 0))
    return pl.pallas_call(
        functools.partial(products, n, layer),
        grid=(layer,),
        out_shape=[
            jax.ShapeDtypeStruct((layer, dof, configs), bf16),
            jax.ShapeDtypeStruct(phi.shape, bf16),
        ],
        in_specs=[
            SMEM,
            SMEM,
            pl.BlockSpec((1, dof, 2 * configs), lambda c: (c, 0, 0)),
            whole,
            whole,
        ],
        out_specs=[
            pl.BlockSpec((1, dof, configs), lambda c: (c, 0, 0)),
            pl.BlockSpec((1, blocks, dof, dof), lambda c: (c, 0, 0, 0)),
        ],
        compiler_params=pltpu.CompilerParams(vmem_limit_bytes=32 * 1024 * 1024),
    )(neighbours, position, sides, frame_disp, frame_resid)


def solution(mesh):
    in_specs = (
        P(("groups", "cx"), None, None),
        P(("groups", "cx"), None, None),
        P(("groups", "cx"), None, None, None),
        P("cx", None),
        P("cx", None),
        P("groups"),
        P("groups"),
    )
    out_specs = (P(("groups", "cx"), None, None), P(("groups", "cx"), None, None, None))
    return jax.shard_map(
        functools.partial(shards, mesh.shape["cx"]),
        mesh=mesh,
        in_specs=in_specs,
        out_specs=out_specs,
        check_vma=False,
    )
```

time: 140 us -> 71.2 us (0.51); the launches traced: 138 us -> 70.8 us
  local copies, waits for them, and re-layouts: 82 us -> 7.76 us
  Pallas kernels: 0 us -> 62.4 us
  matrix products: 25.8 us -> 0 us
  starting transfers between devices: 21.9 us -> 0 us
  waiting for transfers between devices: 4.59 us -> 0 us
  other arithmetic: 3.08 us -> 0 us
    pallas_call x0 -> x2, Pallas kernels: none -> 62.4 us  [the longest x1 55.7 us: shards(): pl.pallas_call(functools.partial(exchange, n, rows, span), out_shape=[fra...]
    unnamed x21 -> x14, local copies, waits for them, and re-layouts: 50.4 us -> 7.76 us
    dot_general x3 -> x0, matrix products: 25.8 us -> none  [the longest x1 11.6 us: shards(): jnp.einsum('cis,ckjs->ckij', wdisp, beside_resid, preferred_element_type=...]
    gather x4 -> x0, local copies, waits for them, and re-layouts: 18.1 us -> none  [the longest x1 6.73 us: shards(): beside_disp = jnp.take(framed_disp, near_index, axis=0)]
    all_to_all x4 -> x0, local copies, waits for them, and re-layouts: 13.2 us -> none  [the longest x2 6.59 us: shards(): lax.all_to_all(forces, 'cx', split_axis=2, concat_axis=0, tiled=True)]
    all_to_all x2 -> x0, starting transfers between devices: 12.9 us -> none  [the longest x1 7.52 us: shards(): lax.all_to_all(displacements, 'cx', split_axis=2, concat_axis=0, tiled=True)]
    ppermute x4 -> x0, starting transfers between devices: 8.92 us -> none  [the longest x2 8.92 us: with_halo(): lax.ppermute(lax.slice_in_dim(block, 0, width, axis=dim), axis, backward)]
    ppermute x4 -> x0, waiting for transfers between devices: 3.98 us -> none  [the longest x2 3.98 us: with_halo(): lax.ppermute(lax.slice_in_dim(block, block.shape[dim] - width, None, axis...]
  transfers between devices with their start and end apart: 6 -> 0, of which waited for: 2 -> 0; matrix products, arithmetic and copies ran while one was open for 38% -> 0% of each run, Pallas kernels for 0% -> 0%
where the time goes in v1:
time: 71.2 us; the launch traced here: 70.8 us
  Pallas kernels  62.4 us (88%)
  local copies, waits for them, and re-layouts  7.76 us (11%)
    pallas_call x1, Pallas kernels, shards(): pl.pallas_call(functools.partial(exchange, n, rows, span), out_shape=[fra...  55.7 us
    unnamed x14, local copies, waits for them, and re-layouts  7.76 us
    pallas_call x1, Pallas kernels, shards(): pl.pallas_call(functools.partial(products, n, layer), grid=(layer,), out_...  6.65 us

profile of v1, /device:TPU:0, one launch (start us, length us, event | category | flops | bytes accessed | tf_op | source)
XLA Modules:
  0.0 70.8 jit_solution(11745078775098695785)
XLA Ops:
  0.6 0.0 copy-start
  0.6 3.0 %copy-done = bf16[5,14,192,192]{3,2,1,0:T(8,128)(2,1)S(1)} copy-done((bf16[5,14,192,192]{3,2,1,0:T(8,128)(2,1)S(1)}, bf16[5,14,192,192]{3,2,1,0:T(8,128)(2,1)}, u32[]{:S(2)}) %copy-start) | copy-done | bytes 5160984
  3.6 0.0 copy-start.1
  3.6 1.0 %copy-done.1 = bf16[16,3,5120]{2,0,1:T(8,128)(2,1)S(1)} copy-done((bf16[16,3,5120]{2,0,1:T(8,128)(2,1)S(1)}, bf16[16,3,5120]{2,0,1:T(8,128)(2,1)}, u32[]{:S(2)}) %copy-start.1) | copy-done | bytes 491544
  4.6 0.0 copy-start.2
  4.6 1.0 %copy-done.2 = bf16[16,3,5120]{2,0,1:T(8,128)(2,1)S(1)} copy-done((bf16[16,3,5120]{2,0,1:T(8,128)(2,1)S(1)}, bf16[16,3,5120]{2,0,1:T(8,128)(2,1)}, u32[]{:S(2)}) %copy-start.2) | copy-done | bytes 491544
  5.7 0.0 copy-start.3
  5.7 0.7 copy-done.3
  6.4 0.0 copy-start.4
  6.4 0.7 copy-done.4
  7.1 0.0 copy-start.5
  7.1 0.7 copy-done.5
  7.7 0.0 copy-start.6
  7.7 0.7 copy-done.6
  8.4 55.7 %shard_map.86 = (bf16[15,192,256]{2,1,0:T(8,128)(2,1)S(1)}, bf16[15,192,256]{2,1,0:T(8,128)(2,1)S(1)}, bf16[5,192,512]{2,1,0:T(8,128)(2,1)S(1)}) custom-call(bf16[3,16,5120]{2,1,0:T(8,128)(2,1)S(1)} %bitcast.5, bf16[3,16,5120]{2,1,0:T(8,128)(2,1)S(1)} %bitcast.6, bf16[5,14,192,192]{3,2,1,0:T(8,128)(2,1)S(1)} %copy-done, s32[5,14]{1,0:T(8,128)S(1)} %copy-done.3, ...), custom_call_target="tpu_custom_call" | custom-call | tf_op jit(solution)/shard_map/pallas_call | solution.py:230
  64.2 6.7 %shard_map.87 = (bf16[5,192,256]{2,1,0:T(8,128)(2,1)}, bf16[5,14,192,192]{3,2,1,0:T(8,128)(2,1)}) custom-call(s32[5,14]{1,0:T(8,128)S(1)} %copy-done.3, s32[1]{0:T(128)} %bitcast.position, bf16[5,192,512]{2,1,0:T(8,128)(2,1)S(1)} %get-tuple-element.5.sides, bf16[15,192,256]{2,1,0:T(8,128)(2,1)S(1)} %get-tuple-element.6.disp, ...), custom_call_target="tpu_custom_call" | custom-call | tf_op jit(solution)/shard_map/pallas_call | solution.py:268
Async XLA Ops:
  0.6 3.0 %copy-start = (bf16[5,14,192,192]{3,2,1,0:T(8,128)(2,1)S(1)}, bf16[5,14,192,192]{3,2,1,0:T(8,128)(2,1)}, u32[]{:S(2)}) copy-start(bf16[5,14,192,192]{3,2,1,0:T(8,128)(2,1)} %phi.1) | copy-start | bytes 15482884
  3.6 1.0 %copy-start.1 = (bf16[16,3,5120]{2,0,1:T(8,128)(2,1)S(1)}, bf16[16,3,5120]{2,0,1:T(8,128)(2,1)}, u32[]{:S(2)}) copy-start(bf16[16,3,5120]{2,0,1:T(8,128)(2,1)} %param.7) | copy-start | bytes 1474564
  4.6 1.0 %copy-start.2 = (bf16[16,3,5120]{2,0,1:T(8,128)(2,1)S(1)}, bf16[16,3,5120]{2,0,1:T(8,128)(2,1)}, u32[]{:S(2)}) copy-start(bf16[16,3,5120]{2,0,1:T(8,128)(2,1)} %param.8) | copy-start | bytes 1474564
  5.7 0.7 copy-start.3
  6.4 0.7 copy-start.4
  7.1 0.7 copy-start.5
  7.7 0.7 copy-start.6

commit v2 on v1

--- a/solution.py
+++ b/solution.py
@@ -25,68 +25,121 @@
 
 def exchange(
     n, rows, span,
-    disp, force, phi, near, atoms, order, weights,
+    disp, force, phi, near_in, atoms_in, order_in, weights_in,
     frame_disp, frame_resid, sides,
-    phi_v, got_disp, got_force, pick, cdisp, cforce, resid, wt,
-    own_sem, phi_sem, send_sem, recv_sem, halo_send, halo_recv, back_send, back_recv, out_sem,
+    near, atoms, order, weights,
+    phi_v, raw_disp, raw_force, made_disp, made_force, got_disp, got_force, pick, cdisp, cforce, resid, wt, small_sem,
+    raw_sem, own_sem, phi_sem, send_sem, recv_sem, halo_send, halo_recv, back_send, back_recv, out_sem,
 ):
     layer, size = atoms.shape
     blocks = phi.shape[1]
-    padded, width = got_disp.shape[2:]
+    slots, padded = got_disp.shape[1:3]
+    full = (slots - 2) // 3
+    edge = full * LANES
+    half = LANES // 2
     me = lax.axis_index("cx")
     right, left = lax.rem(me + 1, n), lax.rem(me + n - 1, n)
 
-    def start_of(owner):
-        return pl.multiple_of((owner * span) // LANES * LANES, LANES)
-
     phi_copies = [
         pltpu.make_async_copy(phi.at[c], phi_v.at[c], phi_sem.at[c]) for c in range(layer)
     ]
-    fields = ((disp, got_disp), (force, got_force))
+    fields = ((raw_disp, made_disp, got_disp), (raw_force, made_force, got_force))
+    raw_copies = [
+        pltpu.make_async_copy(src, fields[i][0], raw_sem.at[i]) for i, src in enumerate((disp, force))
+    ]
     own_copies = [
-        pltpu.make_async_copy(src.at[:, :, pl.ds(start_of(me), width)], dst.at[me], own_sem.at[i])
-        for i, (src, dst) in enumerate(fields)
-    ]
-
+        pltpu.make_async_copy(made.at[me], got.at[me], own_sem.at[i])
+        for i, (_, made, got) in enumerate(fields)
+    ]
+    small_copies = [
+        pltpu.make_async_copy(src, dst, small_sem.at[i])
+        for i, (src, dst) in enumerate(
+            ((near_in, near), (atoms_in, atoms), (order_in, order), (weights_in, weights))
+        )
+    ]
     barrier = pltpu.get_barrier_semaphore()
 
     @pl.loop(1, n)
     def _(i):
         pl.semaphore_signal(barrier, inc=1, device_id={"cx": lax.rem(me + i, n)})
 
-    for copy in own_copies:
+    for copy in raw_copies + small_copies:
         copy.start()
 
-    shift = me * span - (me * span) // LANES * LANES
+    lane = lax.broadcasted_iota(jnp.int32, (padded, LANES), 1)
+
+    def pack(field):
+        raw, made, _ = fields[field]
+
+        @pl.loop(0, n // 2)
+        def _(pair):
+            base = pair * (2 * span)
+
+            def tile(a, t):
+                return raw[a, :, pl.ds(pl.multiple_of(base + t * LANES, LANES), LANES)]
+
+            for a in range(3):
+                for t in range(full):
+                    made[2 * pair, a * full + t] = tile(a, t)
+                    made[2 * pair + 1, a * full + t] = tile(a, full + 1 + t)
+            first = tile(0, full).astype(jnp.float32)
+            second = pltpu.roll(tile(1, full).astype(jnp.float32), half, 1)
+            third = tile(2, full)
+            made[2 * pair, 3 * full] = jnp.where(lane < half, first, second).astype(jnp.bfloat16)
+            made[2 * pair + 1, 3 * full] = jnp.where(lane < half, second, first).astype(jnp.bfloat16)
+            made[2 * pair, 3 * full + 1] = third
+            made[2 * pair + 1, 3 * full + 1] = third
+
+    def moved(field, i, owner):
+        _, made, got = fields[field]
+        peer = lax.rem(me + i, n)
+        return pltpu.make_async_remote_copy(
+            src_ref=made.at[peer],
+            dst_ref=got.at[owner],
+            send_sem=send_sem.at[field, i],
+            recv_sem=recv_sem.at[field, i],
+            device_id={"cx": peer},
+        )
+
+    raw_copies[0].wait()
+    pack(0)
+    pl.semaphore_wait(barrier, n - 1)
+
+    @pl.loop(1, n)
+    def _(i):
+        moved(0, i, me).start()
+
+    own_copies[0].start()
+    for copy in phi_copies:
+        copy.start()
+    raw_copies[1].wait()
+    pack(1)
+    own_copies[1].start()
+
+    for copy in small_copies:
+        copy.wait()
+    width = pick.shape[2]
+    odd = lax.rem(me, 2)
+    at = lax.broadcasted_iota(jnp.int32, (size, width), 1).astype(jnp.float32)
     for c in range(layer):
-        place = column((atoms[c : c + 1, :] - me * span + shift).astype(jnp.float32))
-        lane = lax.broadcasted_iota(jnp.int32, (size, width), 1).astype(jnp.float32)
-        pick[c * size : (c + 1) * size, :] = jnp.where(lane == place, 1.0, 0.0).astype(jnp.bfloat16)
+        local = atoms[c : c + 1, :] - me * span
+        moved_on = jnp.where(local < half, local + (edge + half), local - half)
+        place = jnp.where(odd == 1, moved_on, local)
+        other = jnp.where(
+            place >= edge, jnp.where(place >= edge + half, place - half, place + half), place
+        )
+        for i, row in enumerate((place, other)):
+            pick[i, c * size : (c + 1) * size, :] = jnp.where(
+                at == column(row.astype(jnp.float32)), 1.0, 0.0
+            ).astype(jnp.bfloat16)
     configs = order.shape[1]
     match = order[...] == lax.broadcasted_iota(jnp.int32, (configs, configs), 0)
     wt[...] = jnp.sum(jnp.where(match, column(weights[...]), 0.0), axis=0, keepdims=True)
 
-    pl.semaphore_wait(barrier, n - 1)
-
-    def moved(field, i, owner):
-        src, dst = fields[field]
-        peer = lax.rem(me + i, n)
-        return pltpu.make_async_remote_copy(
-            src_ref=src.at[:, :, pl.ds(start_of(peer), width)],
-            dst_ref=dst.at[owner],
-            send_sem=send_sem.at[field, i],
-            recv_sem=recv_sem.at[field, i],
-            device_id={"cx": peer},
-        )
-
-    for field in range(2):
-
-        @pl.loop(1, n)
-        def _(i):
-            moved(field, i, me).start()
-
-    for copy in phi_copies:
-        copy.start()
+    @pl.loop(1, n)
+    def _(i):
+        moved(0, i, me).wait_send()
+        moved(1, i, me).start()
 
     def gathered(field, store):
         own_copies[field].wait()
@@ -96,8 +149,10 @@
             moved(field, i, lax.rem(me + n - i, n)).wait_recv()
 
         for a in range(3):
-            x = fields[field][1][:, a].reshape(n * padded, width)
-            y = lax.dot_general(pick[...], x, NT, preferred_element_type=jnp.float32)
+            got = fields[field][2]
+            tiles = [a * full + t for t in range(full)] + [3 * full + a // 2]
+            x = jnp.concatenate([got[:, t].reshape(n * padded, LANES) for t in tiles], axis=1)
+            y = lax.dot_general(pick[a % 2], x, NT, preferred_element_type=jnp.float32)
             if padded != rows:
                 sub = lax.broadcasted_iota(jnp.int32, (n * padded, n * rows), 0)
                 col = lax.broadcasted_iota(jnp.int32, (n * padded, n * rows), 1)
@@ -174,11 +229,9 @@
             jnp.bfloat16
         )
 
-    for field in range(2):
-
-        @pl.loop(1, n)
-        def _(i):
-            moved(field, i, me).wait_send()
+    @pl.loop(1, n)
+    def _(i):
+        moved(1, i, me).wait_send()
 
     for copy in halo:
         copy.wait_send()
@@ -213,9 +266,9 @@
     blocks, dof = phi.shape[1:3]
     configs = config_order.shape[0]
     span = atoms // n
-    width = -(-span // LANES) * LANES
-    while any((p * span) % LANES + span > width for p in range(n)):
-        width += LANES
+    full, rest = divmod(span, LANES)
+    assert 2 * rest == LANES and n % 2 == 0
+    slots, width = 3 * full + 2, (full + 1) * LANES
     padded = -(-rows // SUBLANES) * SUBLANES
 
     def laid(field):
@@ -230,17 +283,23 @@
     frame_disp, frame_resid, sides = pl.pallas_call(
         functools.partial(exchange, n, rows, span),
         out_shape=[frame, frame, jax.ShapeDtypeStruct((layer, dof, 2 * configs), bf16)],
-        in_specs=[ANY, ANY, ANY, SMEM, VMEM, VMEM, VMEM],
+        in_specs=[ANY] * 7,
         out_specs=[ANY, ANY, VMEM],
         scratch_shapes=[
+            pltpu.SMEM(neighbours.shape, jnp.int32),
+            pltpu.VMEM(cluster_atoms.shape, jnp.int32),
+            pltpu.VMEM((1, configs), jnp.int32),
+            pltpu.VMEM((1, configs), jnp.float32),
             pltpu.VMEM(phi.shape, bf16),
-            pltpu.VMEM((n, 3, padded, width), bf16),
-            pltpu.VMEM((n, 3, padded, width), bf16),
-            pltpu.VMEM((layer * size, width), bf16),
+            *[pltpu.VMEM((3, padded, atoms), bf16)] * 2,
+            *[pltpu.VMEM((n, slots, padded, LANES), bf16)] * 4,
+            pltpu.VMEM((2, layer * size, width), bf16),
             pltpu.VMEM((3 * layer, dof, configs), bf16),
             pltpu.VMEM((layer, dof, configs), jnp.float32),
             pltpu.VMEM((layer, dof, configs), bf16),
             pltpu.VMEM((1, configs), jnp.float32),
+            dma((4,)),
+            dma((2,)),
             dma((2,)),
             dma((layer,)),
             dma((2, n)),
@@ -252,7 +311,7 @@
             dma((1 + layer,)),
         ],
         compiler_params=pltpu.CompilerParams(
-            collective_id=0, has_side_effects=True, vmem_limit_bytes=32 * 1024 * 1024
+            collective_id=0, has_side_effects=True, vmem_limit_bytes=60 * 1024 * 1024
         ),
     )(
         laid(displacements),
@@ -283,7 +342,7 @@
             pl.BlockSpec((1, dof, configs), lambda c: (c, 0, 0)),
             pl.BlockSpec((1, blocks, dof, dof), lambda c: (c, 0, 0, 0)),
         ],
-        compiler_params=pltpu.CompilerParams(vmem_limit_bytes=32 * 1024 * 1024),
+        compiler_params=pltpu.CompilerParams(vmem_limit_bytes=60 * 1024 * 1024),
     )(neighbours, position, sides, frame_disp, frame_resid)
 
 

time: 71.2 us -> 58.4 us (0.82)
  the two profiles are of different devices: /device:TPU:0 before, /device:TPU:12 now
where the time goes in v2:
time: 58.4 us; the launch traced here: 58.1 us
  Pallas kernels  57.5 us (98%)
  between operations  0.64 us (1%)
    pallas_call x1, Pallas kernels, shards(): pl.pallas_call(functools.partial(exchange, n, rows, span), out_shape=[fra...  49.3 us
    pallas_call x1, Pallas kernels, shards(): pl.pallas_call(functools.partial(products, n, layer), grid=(layer,), out_...  8.22 us

profile of v2, /device:TPU:12, one launch (start us, length us, event | category | flops | bytes accessed | tf_op | source)
XLA Modules:
  0.0 58.1 jit_solution(8745159408769580012)
XLA Ops:
  0.6 49.3 %shard_map.86 = (bf16[15,192,256]{2,1,0:T(8,128)(2,1)}, bf16[15,192,256]{2,1,0:T(8,128)(2,1)}, bf16[5,192,512]{2,1,0:T(8,128)(2,1)}) custom-call(bf16[3,16,5120]{2,1,0:T(8,128)(2,1)} %bitcast.5, bf16[3,16,5120]{2,1,0:T(8,128)(2,1)} %bitcast.6, bf16[5,14,192,192]{3,2,1,0:T(8,128)(2,1)} %phi.1, s32[5,14]{1,0:T(8,128)} %near.1, s32[5,64]{1,0:T(8,128)} %atoms_in.1, ...), custom_call_target="tpu_custom_call" | custom-call | tf_op jit(solution)/shard_map/pallas_call | solution.py:283
  49.9 8.2 %shard_map.87 = (bf16[5,192,256]{2,1,0:T(8,128)(2,1)}, bf16[5,14,192,192]{3,2,1,0:T(8,128)(2,1)}) custom-call(s32[5,14]{1,0:T(8,128)} %near.1, s32[1]{0:T(128)} %bitcast.position, bf16[5,192,512]{2,1,0:T(8,128)(2,1)} %get-tuple-element.5.sides, bf16[15,192,256]{2,1,0:T(8,128)(2,1)} %get-tuple-element.6.disp, bf16[15,192,256]{2,1,0:T(8,128)(2,1)} %get-tuple-element.7.resid), custom_call_target="tpu_custom_call" | custom-call | tf_op jit(solution)/shard_map/pallas_call | solution.py:327

commit v3 on v2

--- a/solution.py
+++ b/solution.py
@@ -26,10 +26,10 @@
 def exchange(
     n, rows, span,
     disp, force, phi, near_in, atoms_in, order_in, weights_in,
-    frame_disp, frame_resid, sides,
+    frame_resid, sides, part_out,
     near, atoms, order, weights,
-    phi_v, raw_disp, raw_force, made_disp, made_force, got_disp, got_force, pick, cdisp, cforce, resid, wt, small_sem,
-    raw_sem, own_sem, phi_sem, send_sem, recv_sem, halo_send, halo_recv, back_send, back_recv, out_sem,
+    phi_v, part, raw_disp, raw_force, made_disp, made_force, got_disp, got_force, pick, cdisp, cforce, resid, wt, small_sem,
+    raw_sem, own_sem, phi_sem, send_sem, recv_sem, halo_send, halo_recv, back_send, back_recv, out_sem, part_sem,
 ):
     layer, size = atoms.shape
     blocks = phi.shape[1]
@@ -188,8 +188,6 @@
     gathered(1, keep_force)
     for copy in halo:
         copy.wait_recv()
-    disp_out = pltpu.make_async_copy(cdisp, frame_disp, out_sem.at[0])
-    disp_out.start()
     for copy in phi_copies:
         copy.wait()
 
@@ -204,30 +202,36 @@
         )
 
     def keep(c):
-        return pltpu.make_async_copy(resid.at[c], frame_resid.at[layer + c], out_sem.at[1 + c])
-
-    dof = 3 * size
+        return pltpu.make_async_copy(resid.at[c], frame_resid.at[layer + c], out_sem.at[c])
+
+    def beside(c, k):
+        name = near[c, k]
+        offset = jnp.minimum(lax.rem(name // layer - me + 1 + n, n), 2)
+        return cdisp[offset * layer + lax.rem(name, layer)]
 
     @pl.loop(0, layer)
     def _(c):
         total = cforce[c]
         for k in range(blocks):
-            name = near[c, k]
-            offset = jnp.minimum(lax.rem(name // layer - me + 1 + n, n), 2)
-            total += jnp.dot(
-                phi_v[c, k],
-                cdisp[offset * layer + lax.rem(name, layer)],
-                preferred_element_type=jnp.float32,
-            )
+            total += jnp.dot(phi_v[c, k], beside(c, k), preferred_element_type=jnp.float32)
         rounded = total.astype(jnp.bfloat16)
         resid[c] = rounded
         back(c, 0).start()
         back(c, 1).start()
         keep(c).start()
-        sides[c, :, :configs] = (rounded.astype(jnp.float32) * wt[...]).astype(jnp.bfloat16)
-        sides[c, :, configs:] = (cdisp[layer + c].astype(jnp.float32) * wt[...]).astype(
-            jnp.bfloat16
-        )
+
+    def part_copy(c):
+        return pltpu.make_async_copy(part.at[c], part_out.at[c], part_sem.at[c])
+
+    @pl.loop(0, layer)
+    def _(c):
+        wres = (resid[c].astype(jnp.float32) * wt[...]).astype(jnp.bfloat16)
+        sides[c] = (cdisp[layer + c].astype(jnp.float32) * wt[...]).astype(jnp.bfloat16)
+        for k in range(blocks):
+            part[c, k] = lax.dot_general(
+                wres, beside(c, k), NT, preferred_element_type=jnp.float32
+            ).astype(jnp.bfloat16)
+        part_copy(c).start()
 
     @pl.loop(1, n)
     def _(i):
@@ -235,27 +239,24 @@
 
     for copy in halo:
         copy.wait_send()
-    disp_out.wait()
     for c in range(layer):
         keep(c).wait()
+        part_copy(c).wait()
         for side in range(2):
             back(c, side).wait()
 
 
-def products(n, layer, near, position, sides, disp, resid, residual, gradient):
+def products(n, layer, near, position, sides, part, resid, residual, gradient):
     c = pl.program_id(0)
     blocks = gradient.shape[1]
-    configs = disp.shape[2]
     me = position[0]
     residual[0] = resid[layer + c]
     for k in range(blocks):
         name = near[c, k]
         offset = jnp.minimum(lax.rem(name // layer - me + 1 + n, n), 2)
         index = offset * layer + lax.rem(name, layer)
-        total = lax.dot_general(
-            sides[0, :, :configs], disp[index], NT, preferred_element_type=jnp.float32
-        ) + lax.dot_general(
-            sides[0, :, configs:], resid[index], NT, preferred_element_type=jnp.float32
+        total = part[0, k].astype(jnp.float32) + lax.dot_general(
+            sides[0], resid[index], NT, preferred_element_type=jnp.float32
         )
         gradient[0, k] = (0.5 * total).astype(jnp.bfloat16)
 
@@ -280,17 +281,21 @@
     bf16 = jnp.bfloat16
     dma = pltpu.SemaphoreType.DMA
     frame = jax.ShapeDtypeStruct((3 * layer, dof, configs), bf16)
-    frame_disp, frame_resid, sides = pl.pallas_call(
+    frame_resid, sides, part = pl.pallas_call(
         functools.partial(exchange, n, rows, span),
-        out_shape=[frame, frame, jax.ShapeDtypeStruct((layer, dof, 2 * configs), bf16)],
+        out_shape=[
+            frame,
+            jax.ShapeDtypeStruct((layer, dof, configs), bf16),
+            jax.ShapeDtypeStruct(phi.shape, bf16),
+        ],
         in_specs=[ANY] * 7,
-        out_specs=[ANY, ANY, VMEM],
+        out_specs=[ANY, VMEM, ANY],
         scratch_shapes=[
             pltpu.SMEM(neighbours.shape, jnp.int32),
             pltpu.VMEM(cluster_atoms.shape, jnp.int32),
             pltpu.VMEM((1, configs), jnp.int32),
             pltpu.VMEM((1, configs), jnp.float32),
-            pltpu.VMEM(phi.shape, bf16),
+            *[pltpu.VMEM(phi.shape, bf16)] * 2,
             *[pltpu.VMEM((3, padded, atoms), bf16)] * 2,
             *[pltpu.VMEM((n, slots, padded, LANES), bf16)] * 4,
             pltpu.VMEM((2, layer * size, width), bf16),
@@ -308,7 +313,8 @@
             dma((2,)),
             dma((2, layer)),
             dma((2, layer)),
-            dma((1 + layer,)),
+            dma((layer,)),
+            dma((layer,)),
         ],
         compiler_params=pltpu.CompilerParams(
             collective_id=0, has_side_effects=True, vmem_limit_bytes=60 * 1024 * 1024
@@ -323,7 +329,6 @@
         weights.reshape(1, configs),
     )
     position = lax.axis_index("cx").reshape(1).astype(jnp.int32)
-    whole = pl.BlockSpec((3 * layer, dof, configs), lambda c: (0, 0, 0))
     return pl.pallas_call(
         functools.partial(products, n, layer),
         grid=(layer,),
@@ -334,16 +339,16 @@
         in_specs=[
             SMEM,
             SMEM,
-            pl.BlockSpec((1, dof, 2 * configs), lambda c: (c, 0, 0)),
-            whole,
-            whole,
+            pl.BlockSpec((1, dof, configs), lambda c: (c, 0, 0)),
+            pl.BlockSpec((1, blocks, dof, dof), lambda c: (c, 0, 0, 0)),
+            pl.BlockSpec((3 * layer, dof, configs), lambda c: (0, 0, 0)),
         ],
         out_specs=[
             pl.BlockSpec((1, dof, configs), lambda c: (c, 0, 0)),
             pl.BlockSpec((1, blocks, dof, dof), lambda c: (c, 0, 0, 0)),
         ],
         compiler_params=pltpu.CompilerParams(vmem_limit_bytes=60 * 1024 * 1024),
-    )(neighbours, position, sides, frame_disp, frame_resid)
+    )(neighbours, position, sides, part, frame_resid)
 
 
 def solution(mesh):

time: 58.4 us -> 59.6 us (1.021)
  Pallas kernels: 57.5 us -> 58.8 us
    pallas_call x1, Pallas kernels: 8.22 us -> 9.55 us  [shards(): pl.pallas_call(functools.partial(products, n, layer), grid=(layer,), out_...]
where the time goes in v3:
time: 59.6 us; the launch traced here: 59.4 us
  Pallas kernels  58.8 us (99%)
  between operations  0.64 us (1%)
    pallas_call x1, Pallas kernels, shards(): pl.pallas_call(functools.partial(exchange, n, rows, span), out_shape=[fra...  49.2 us
    pallas_call x1, Pallas kernels, shards(): pl.pallas_call(functools.partial(products, n, layer), grid=(layer,), out_...  9.55 us

profile of v3, /device:TPU:12, one launch (start us, length us, event | category | flops | bytes accessed | tf_op | source)
XLA Modules:
  0.0 59.4 jit_solution(63345969572504021)
XLA Ops:
  0.6 49.2 %shard_map.86 = (bf16[15,192,256]{2,1,0:T(8,128)(2,1)}, bf16[5,192,256]{2,1,0:T(8,128)(2,1)}, bf16[5,14,192,192]{3,2,1,0:T(8,128)(2,1)}) custom-call(bf16[3,16,5120]{2,1,0:T(8,128)(2,1)} %bitcast.5, bf16[3,16,5120]{2,1,0:T(8,128)(2,1)} %bitcast.6, bf16[5,14,192,192]{3,2,1,0:T(8,128)(2,1)} %phi.1, s32[5,14]{1,0:T(8,128)} %near.1, s32[5,64]{1,0:T(8,128)} %atoms_in.1, ...), custom_call_target="tpu_custom_call" | custom-call | tf_op jit(solution)/shard_map/pallas_call | solution.py:284
  49.9 9.5 %shard_map.87 = (bf16[5,192,256]{2,1,0:T(8,128)(2,1)}, bf16[5,14,192,192]{3,2,1,0:T(8,128)(2,1)}) custom-call(s32[5,14]{1,0:T(8,128)} %near.1, s32[1]{0:T(128)} %bitcast.position, bf16[5,192,256]{2,1,0:T(8,128)(2,1)} %get-tuple-element.5.sides, bf16[5,14,192,192]{3,2,1,0:T(8,128)(2,1)} %get-tuple-element.6.part, bf16[15,192,256]{2,1,0:T(8,128)(2,1)} %get-tuple-element.7.resid), custom_call_target="tpu_custom_call" | custom-call | tf_op jit(solution)/shard_map/pallas_call | solution.py:332

commit v4 on v2

--- a/solution.py
+++ b/solution.py
@@ -136,7 +136,7 @@
     match = order[...] == lax.broadcasted_iota(jnp.int32, (configs, configs), 0)
     wt[...] = jnp.sum(jnp.where(match, column(weights[...]), 0.0), axis=0, keepdims=True)
 
-    @pl.loop(1, n)
+    @pl.loop(1, n // 2)
     def _(i):
         moved(0, i, me).wait_send()
         moved(1, i, me).start()
@@ -185,6 +185,12 @@
     ]
     for copy in halo:
         copy.start()
+
+    @pl.loop(n // 2, n)
+    def _(i):
+        moved(0, i, me).wait_send()
+        moved(1, i, me).start()
+
     gathered(1, keep_force)
     for copy in halo:
         copy.wait_recv()

time: 58.4 us -> 59.7 us (1.022)
  the two profiles are of different devices: /device:TPU:12 before, /device:TPU:1 now
where the time goes in v4:
time: 59.7 us; the launch traced here: 59.5 us
  Pallas kernels  58.8 us (98%)
  between operations  0.64 us (1%)
    pallas_call x1, Pallas kernels, shards(): pl.pallas_call(functools.partial(exchange, n, rows, span), out_shape=[fra...  50.6 us
    pallas_call x1, Pallas kernels, shards(): pl.pallas_call(functools.partial(products, n, layer), grid=(layer,), out_...  8.22 us

profile of v4, /device:TPU:1, one launch (start us, length us, event | category | flops | bytes accessed | tf_op | source)
XLA Modules:
  0.0 59.5 jit_solution(13234521803599704054)
XLA Ops:
  0.6 50.6 %shard_map.86 = (bf16[15,192,256]{2,1,0:T(8,128)(2,1)}, bf16[15,192,256]{2,1,0:T(8,128)(2,1)}, bf16[5,192,512]{2,1,0:T(8,128)(2,1)}) custom-call(bf16[3,16,5120]{2,1,0:T(8,128)(2,1)} %bitcast.5, bf16[3,16,5120]{2,1,0:T(8,128)(2,1)} %bitcast.6, bf16[5,14,192,192]{3,2,1,0:T(8,128)(2,1)} %phi.1, s32[5,14]{1,0:T(8,128)} %near.1, s32[5,64]{1,0:T(8,128)} %atoms_in.1, ...), custom_call_target="tpu_custom_call" | custom-call | tf_op jit(solution)/shard_map/pallas_call | solution.py:289
  51.3 8.2 %shard_map.87 = (bf16[5,192,256]{2,1,0:T(8,128)(2,1)}, bf16[5,14,192,192]{3,2,1,0:T(8,128)(2,1)}) custom-call(s32[5,14]{1,0:T(8,128)} %near.1, s32[1]{0:T(128)} %bitcast.position, bf16[5,192,512]{2,1,0:T(8,128)(2,1)} %get-tuple-element.5.sides, bf16[15,192,256]{2,1,0:T(8,128)(2,1)} %get-tuple-element.6.disp, bf16[15,192,256]{2,1,0:T(8,128)(2,1)} %get-tuple-element.7.resid), custom_call_target="tpu_custom_call" | custom-call | tf_op jit(solution)/shard_map/pallas_call | solution.py:333
